TPU v7x, 256 devices: a whole 4x4x8 slice. The times are simulated.
256 devices in a mesh: lat: 16 (over z, x_lo), lon: 16 (over x_hi, y, core).
Axes of the slice: x: 4 (x_hi: 2, x_lo: 2; x = x_hi * 2 + x_lo), y: 4, z: 8, core: 2. Of those that a mesh axis runs over, the one named last changes fastest.
Arguments:
- state: bfloat16 [64, 128, 64, 128], P('lat', 'lon'), may hold values from -6 to 6
- obs_row: int32 [64, 128, 128], P('lat', 'lon'), may hold values from 0 to 63
- obs_count: int32 [64, 128], P('lat', 'lon'), may hold values from 0 to 128
- obs_value: float32 [64, 128, 128], P('lat', 'lon'), may hold values from -6 to 6
- obs_weight: float32 [64, 128, 128], P('lat', 'lon'), may hold values from 0.5 to 2
- quadrant: int32 [64, 128, 64], P('lat', 'lon'), may hold values from 0 to 3
- frac_lat: float32 [64, 128, 64], P('lat', 'lon'), may hold values from 0 to 1
- frac_lon: float32 [64, 128, 64], P('lat', 'lon'), may hold values from 0 to 1
- land: int32 [64, 128, 64], P('lat', 'lon'), may hold values 0 or 1
Outputs:
- analysis: bfloat16 [64, 128, 64, 128], P('lat', 'lon')
All inputs are finite; a program needn't handle non-finite values. No bound on the sum of `land` on one device may be relied on, other than what follows from the above.
Results may differ from a plain program's by a relative error of at most 0.0051.
Values may be sent and summed in bfloat16 or wider, within the bound.
No kernel may reach another device: no remote copies, remote signals or barrier semaphores. Data moves between devices by JAX's collectives and lax.ppermute only.
A program may use at most 64 MiB of HBM per device.

v0:
```python
import math

import jax
import jax.numpy as jnp
from jax import lax
from jax.experimental import pallas as pl
from jax.experimental.pallas import tpu as pltpu
from jax.sharding import PartitionSpec as P

F32 = jnp.float32
BF16 = jnp.bfloat16
ITERS = 6
NEAR = (0.5, 1.0, 0.5)
PARAMS = pltpu.CompilerParams(vmem_limit_bytes=40 * 2**20)


def swap(x, axis, phase):
    count = lax.axis_size(axis)
    pairs = []
    for k in range(phase, count, 2):
        a, b = k, (k + 1) % count
        pairs += [(a, b), (b, a)]
    return lax.ppermute(x, axis, pairs)


def swap_inner_lat(x):
    lats, lons = lax.axis_size("lat"), lax.axis_size("lon")
    pairs = []
    for j in range(lons):
        for k in range(1, lats - 1, 2):
            a, b = k * lons + j, (k + 1) * lons + j
            pairs += [(a, b), (b, a)]
        for k in (0, lats - 1):
            pairs.append((k * lons + j, k * lons + (j ^ 1)))
    return lax.ppermute(x, ("lat", "lon"), pairs)


def split(x):
    high = x.astype(BF16)
    return high, (x - high.astype(F32)).astype(BF16)


def stream(pair):
    return jnp.concatenate(pair, axis=1)


def held(pair):
    row = jnp.concatenate(pair, axis=1)
    return jnp.concatenate([row, row], axis=0)


def product(a, b):
    out = jnp.dot(stream(a), held(b), preferred_element_type=F32)
    half = out.shape[1] // 2
    return out[:, :half] + out[:, half:]


def weights_of(grams, sides):
    members = grams[0].shape[0]
    rows = lax.broadcasted_iota(jnp.int32, (members, members), 0)
    cols = lax.broadcasted_iota(jnp.int32, (members, members), 1)
    eye = jnp.where(rows == cols, F32(1.0), F32(0.0))
    inv_frob = []
    iterates = []
    for gram in grams:
        total = jnp.sum(jnp.sum(gram * gram, axis=0, keepdims=True), axis=1, keepdims=True)
        inverse = lax.rsqrt(total)
        inv_frob.append(inverse)
        iterates.append(gram * inverse)
    first = [split(a) for a in iterates]
    squares, square_parts = iterates, first
    for step in range(0, ITERS, 2):
        inner = [
            product(part, part) + (3.375 * eye - 4.5 * x)
            for part, x in zip(square_parts, squares)
        ]
        inner_parts = [split(x) for x in inner]
        factors = [
            0.0625 * product(part, part) + ((24.609375 / 16) * eye - (8.625 / 16) * x)
            for part, x in zip(inner_parts, squares)
        ]
        factor_parts = [split(x) for x in factors]
        if step == 0:
            roots, root_parts = factors, factor_parts
        else:
            roots = [product(z, x) for z, x in zip(root_parts, factor_parts)]
        if step < ITERS - 2:
            if step > 0:
                root_parts = [split(z) for z in roots]
            half = [split(product(a, z)) for a, z in zip(first, root_parts)]
            squares = [product(x, z) for x, z in zip(half, root_parts)]
            square_parts = [split(x) for x in squares]
    out = []
    for root, side, inverse in zip(roots, sides, inv_frob):
        inner = jnp.sum(root * side, axis=1, keepdims=True)
        mean_weight = jnp.sum(root * inner, axis=0, keepdims=True) * inverse
        out.append((mean_weight + (math.sqrt(members - 1) * jnp.sqrt(inverse)) * root).astype(BF16))
    return out


def row_grams(pairs):
    turned = [pair.T for pair in pairs]
    rows = pairs[0].shape[0] // 2
    half = BF16(0.5)
    out = []
    for p in range(len(pairs) - 1):
        first, second = pairs[p], pairs[p + 1]
        zero = jnp.zeros((rows, first.shape[1]), BF16)
        left = jnp.concatenate([first[:rows] * half, first[rows:], second[:rows] * half, zero], axis=0)
        right = jnp.concatenate([zero, first[rows:] * half, second[:rows], second[rows:] * half], axis=0)
        both = jnp.dot(
            jnp.concatenate(turned[p : p + 2], axis=1),
            jnp.concatenate([left, right], axis=1),
            preferred_element_type=F32,
        )
        members = both.shape[0]
        out += [both[:, :members], both[:, members:]]
    return out


def pair_of(ref, i, j):
    pair = ref[i, j : j + 2]
    return pair.reshape(2 * pair.shape[1], pair.shape[2])


def node_sum(base, gram_ref, i, j):
    return base + 0.5 * (gram_ref[i, j] + gram_ref[i + 2, j]) + gram_ref[i + 1, j]


def near_side(side_ref, i, j):
    total = 0.0
    for a in range(3):
        for b in range(3):
            total = total + NEAR[a] * NEAR[b] * side_ref[i + a, j + b : j + b + 1, :]
    return total


def identity(members):
    rows = lax.broadcasted_iota(jnp.int32, (members, members), 0)
    cols = lax.broadcasted_iota(jnp.int32, (members, members), 1)
    return jnp.where(rows == cols, F32(members - 1), F32(0.0))


def pack_side(ref, at, side):
    high = side.astype(BF16).astype(F32)
    ref[at : at + 2 * side.shape[0], :] = jnp.concatenate([high, side - high], axis=0).astype(BF16)


def unpack_side(ref, at, count):
    both = ref[at : at + 2 * count, :].astype(F32)
    return both[:count] + both[count:]


def cell_copies(first, hbm_refs, refs, sems):
    copies = [pltpu.make_async_copy(hbm_refs[0], refs[0], sems.at[0])]
    for k in range(1, 5):
        source = hbm_refs[k].at[pl.ds(first, 2)]
        copies.append(pltpu.make_async_copy(source, refs[k], sems.at[k]))
    return copies


def cell_scratch(count, state, *rest):
    shapes = [pltpu.SMEM(count.shape, count.dtype)]
    for x in (state, *rest):
        shapes.append(pltpu.VMEM((2, *x.shape[1:]), x.dtype))
    return shapes + [pltpu.SemaphoreType.DMA((5,))]


def cell_rows(first, refs, payload_ref, side_ref):
    count_ref, state_ref, row_ref, value_ref, weight_ref = refs
    _, tile_lon, rows, members = state_ref.shape
    slots = row_ref.shape[2]
    lane = lax.broadcasted_iota(jnp.int32, (1, slots), 1)
    row_ids = lax.broadcasted_iota(jnp.int32, (rows, slots), 0)
    for i in range(2):
        for j in range(tile_lon):
            x = state_ref[i, j].astype(F32)
            mean = jnp.sum(x, axis=1, keepdims=True) * (1.0 / members)
            centred = x - mean
            live = jnp.where(lane < count_ref[first + i, j], weight_ref[i, j : j + 1, :], 0.0)
            hit = row_ids == row_ref[i, j : j + 1, :]
            centre = jnp.sum(jnp.where(hit, mean, 0.0), axis=0, keepdims=True)
            innovation = ((value_ref[i, j : j + 1, :] - centre) * live).astype(BF16).astype(F32)
            square = jnp.sum(jnp.where(hit, live * live, 0.0), axis=1, keepdims=True)
            pull = jnp.sum(jnp.where(hit, live * innovation, 0.0), axis=1, keepdims=True)
            k = i * tile_lon + j
            payload_ref[k * rows : (k + 1) * rows, :] = (centred * jnp.sqrt(square)).astype(BF16)
            side_ref[k : k + 1, :] = jnp.sum(centred * pull, axis=0, keepdims=True)
    pack_side(payload_ref, 2 * tile_lon * rows, side_ref[...])


def in_hbm(arrays):
    return [pltpu.with_memory_space_constraint(x, pltpu.HBM) for x in arrays]


def prepare(state, obs_row, obs_count, obs_value, obs_weight):
    tile_lat, tile_lon, rows, members = state.shape
    half = 2 * tile_lon
    arrays = (obs_count, state, obs_row, obs_value, obs_weight)

    def kernel(*refs):
        hbm_refs, (payload_ref, side_ref), cells, sems = refs[:5], refs[5:7], refs[7:12], refs[12]
        first = (1 - lax.rem(lax.axis_index("lat"), 2)) * (tile_lat - 2)
        copies = cell_copies(first, hbm_refs, cells, sems)
        for copy in copies:
            copy.start()
        for copy in copies:
            copy.wait()
        cell_rows(first, cells, payload_ref, side_ref)

    vmem = pl.BlockSpec(memory_space=pltpu.VMEM)
    return pl.pallas_call(
        kernel,
        in_specs=[pl.BlockSpec(memory_space=pltpu.HBM)] * 5,
        out_specs=[vmem] * 2,
        out_shape=[
            jax.ShapeDtypeStruct((half * rows + 2 * half, members), BF16),
            jax.ShapeDtypeStruct((half, members), F32),
        ],
        scratch_shapes=cell_scratch(*arrays),
        compiler_params=PARAMS,
        cost_estimate=pl.CostEstimate(flops=10**8, bytes_accessed=10**6, transcendentals=0),
        name="prepare",
    )(*in_hbm(arrays))


def complete(state, obs_row, obs_count, obs_value, obs_weight, first_rows, first_side, quadrant, frac_lat, frac_lon, land):
    tile_lat, tile_lon, rows, members = state.shape
    half = 2 * tile_lon
    arrays = (obs_count, state, obs_row, obs_value, obs_weight)
    placing = (quadrant, frac_lat, frac_lon, land)

    def kernel(*refs):
        hbm_refs, placing_hbm, (a_ref, a_side_ref) = refs[:5], refs[5:9], refs[9:11]
        b_ref, q_ref, side_ref, columns_ref, gram_ref = refs[11:16]
        cells, sems = refs[16:21], refs[21]
        b_side_ref, coef_ref = refs[22:24]
        placing_refs, placing_sems = refs[24:28], refs[28]
        quad_ref, flat_ref, flon_ref, land_ref = placing_refs
        odd = lax.rem(lax.axis_index("lat"), 2)
        a_first, b_first = (1 - odd) * (tile_lat - 2), odd * (tile_lat - 2)
        copies = cell_copies(b_first, hbm_refs, cells, sems)
        placing_copies = [
            pltpu.make_async_copy(source, target, placing_sems.at[k])
            for k, (source, target) in enumerate(zip(placing_hbm, placing_refs))
        ]
        for copy in copies + placing_copies:
            copy.start()

        def place(ref, part_ref, first):
            for i in range(2):
                side_ref[first + i] = part_ref[i * tile_lon : (i + 1) * tile_lon]
                pairs = []
                for j in range(0, tile_lon, 2):
                    k = (i * tile_lon + j) * rows
                    q_ref[first + i, j] = ref[k : k + rows, :]
                    q_ref[first + i, j + 1] = ref[k + rows : k + 2 * rows, :]
                    pairs.append(ref[k : k + 2 * rows, :])
                for j, gram in enumerate(row_grams(pairs)):
                    gram_ref[first + i, j] = gram

        place(a_ref, a_side_ref, a_first)
        for copy in copies:
            copy.wait()
        cell_rows(b_first, cells, b_ref, b_side_ref)
        place(b_ref, b_side_ref, b_first)
        coef_ref[...] = jnp.zeros_like(coef_ref)
        for copy in placing_copies:
            copy.wait()

        def columns(i, carry):
            quad = quad_ref[i]
            fa, fo = flat_ref[i], flon_ref[i]
            dry = jnp.where(land_ref[i] == 1, F32(1.0), F32(0.0))
            north, west = quad < 2, lax.rem(quad, 2) == 0
            zero = jnp.zeros_like(fa)
            coefs = (
                jnp.where(north, 1.0 - fa, zero) * dry,
                jnp.where(north, fa, 1.0 - fa) * dry,
                jnp.where(north, zero, fa) * dry,
                jnp.where(west, 1.0 - fo, zero),
                jnp.where(west, fo, 1.0 - fo),
                jnp.where(west, zero, fo),
                dry,
            )
            for k, coef in enumerate(coefs):
                coef_ref[k * tile_lon : (k + 1) * tile_lon, :rows] = coef
            turned = coef_ref[...].T
            for k in range(len(coefs)):
                for j in range(tile_lon):
                    at = k * tile_lon + j
                    columns_ref[i, k, j * rows : (j + 1) * rows, :] = jnp.broadcast_to(
                        turned[:rows, at : at + 1], (rows, members)
                    )
            return carry

        lax.fori_loop(0, tile_lat, columns, 0)

    vmem = pl.BlockSpec(memory_space=pltpu.VMEM)
    return pl.pallas_call(
        kernel,
        in_specs=[pl.BlockSpec(memory_space=pltpu.HBM)] * 9 + [vmem] * 2,
        out_specs=[vmem] * 5,
        out_shape=[
            jax.ShapeDtypeStruct(first_rows.shape, BF16),
            jax.ShapeDtypeStruct(state.shape, BF16),
            jax.ShapeDtypeStruct((tile_lat, tile_lon, members), F32),
            jax.ShapeDtypeStruct((tile_lat, 7, tile_lon * rows, members), F32),
            jax.ShapeDtypeStruct((tile_lat, tile_lon - 2, members, members), F32),
        ],
        scratch_shapes=cell_scratch(*arrays)
        + [pltpu.VMEM((half, members), F32), pltpu.VMEM((128, 128), F32)]
        + [pltpu.VMEM(x.shape, x.dtype) for x in placing]
        + [pltpu.SemaphoreType.DMA((4,))],
        compiler_params=PARAMS,
        cost_estimate=pl.CostEstimate(flops=10**9, bytes_accessed=10**6, transcendentals=0),
        name="complete",
    )(*in_hbm(arrays), *in_hbm(placing), first_rows, first_side)


def interior(side, own_grams):
    tile_lat, tile_lon, members = side.shape

    def kernel(side_ref, gram_ref, out_ref):
        base = identity(members)
        nodes = [(i, j) for i in range(tile_lat - 2) for j in range(tile_lon - 2)]
        sums = [node_sum(base, gram_ref, i, j) for i, j in nodes]
        sides = [near_side(side_ref, i, j) for i, j in nodes]
        for (i, j), w in zip(nodes, weights_of(sums, sides)):
            out_ref[i, j] = w

    vmem = pl.BlockSpec(memory_space=pltpu.VMEM)
    return pl.pallas_call(
        kernel,
        in_specs=[vmem] * 2,
        out_specs=vmem,
        out_shape=jax.ShapeDtypeStruct((tile_lat - 2, tile_lon - 2, members, members), BF16),
        compiler_params=PARAMS,
        cost_estimate=pl.CostEstimate(flops=5 * 10**9, bytes_accessed=2 * 10**6, transcendentals=0),
        name="interior",
    )(side, own_grams)


def lat_edge(phase, side, own_grams, got):
    tile_lat, tile_lon, members = side.shape
    inner = tile_lon - 2
    count = 2 * tile_lon
    rows = got.shape[0] // count - 2

    def kernel(side_ref, own_ref, got_ref, out_ref, near_ref):
        lat = lax.axis_index("lat")
        south = (lax.rem(lat, 2) + phase + 1) % 2
        valid = jnp.where(south == 1, lat < lax.axis_size("lat") - 1, lat > 0)
        got_side = jnp.where(valid, unpack_side(got_ref, count * rows, count), 0.0)
        north_side, south_side = got_side[:tile_lon], got_side[tile_lon:]
        own, behind = south * (tile_lat - 1), 1 + south * (tile_lat - 3)
        near_ref[0] = jnp.where(south == 1, south_side, north_side)
        near_ref[1] = jnp.where(south == 1, north_side, south_side)
        near_ref[2] = side_ref[own]
        near_ref[3] = side_ref[behind]
        grams = []
        for first in (south, 1 - south):
            pairs = []
            for j in range(0, tile_lon, 2):
                start = pl.multiple_of((first * tile_lon + j) * rows, 2 * rows)
                pair = got_ref[pl.ds(start, 2 * rows), :]
                pairs.append(jnp.where(valid, pair, jnp.zeros_like(pair)))
            grams.append(row_grams(pairs))
        far, near = grams
        base = identity(members)
        sums = [base + 0.5 * (far[j] + own_ref[own, j]) + near[j] for j in range(inner)]
        sums += [base + 0.5 * (near[j] + own_ref[behind, j]) + own_ref[own, j] for j in range(inner)]
        sides = [near_side(near_ref, k, j) for k in range(2) for j in range(inner)]
        for n, w in enumerate(weights_of(sums, sides)):
            if n < inner:
                w = jnp.where(valid, w, jnp.zeros_like(w))
            out_ref[n // inner, n % inner] = w

    vmem = pl.BlockSpec(memory_space=pltpu.VMEM)
    return pl.pallas_call(
        kernel,
        in_specs=[vmem] * 3,
        out_specs=vmem,
        out_shape=jax.ShapeDtypeStruct((2, inner, members, members), BF16),
        scratch_shapes=[pltpu.VMEM((4, tile_lon, members), F32)],
        compiler_params=PARAMS,
        cost_estimate=pl.CostEstimate(flops=5 * 10**9, bytes_accessed=2 * 10**6, transcendentals=0),
        name="lat_edge",
    )(side, own_grams, got)


def widen(q, side, got_a, got_b, after):
    tile_lat, tile_lon, rows, members = q.shape
    half = 2 * tile_lon
    wide = tile_lat + 4
    count = 2 * wide
    payload = count * rows + 2 * count

    def kernel(
        q_ref, side_ref, a_ref, b_ref, after_ref, wide_ref, wide_side_ref, to_a_ref, to_b_ref,
    ):
        lat = lax.axis_index("lat")
        lon = lax.axis_index("lon")
        lat_odd = lax.rem(lat, 2)
        lon_odd = lax.rem(lon, 2)
        wide_ref[2 : 2 + tile_lat] = q_ref[...]
        wide_side_ref[2 : 2 + tile_lat] = side_ref[...]
        last = lax.axis_size("lat") - 1
        a_valid = jnp.where(lat_odd == 0, lat < last, lat > 0)
        b_valid = jnp.where(lat_odd == 0, lat > 0, lat < last)
        for ref, first, valid in (
            (a_ref, (1 - lat_odd) * (tile_lat + 2), a_valid),
            (b_ref, lat_odd * (tile_lat + 2), b_valid),
        ):
            total = jnp.where(valid, unpack_side(ref, half * rows, half), 0.0)
            for i in range(2):
                wide_side_ref[first + i] = total[i * tile_lon : (i + 1) * tile_lon]
                for j in range(tile_lon):
                    k = (i * tile_lon + j) * rows
                    piece = ref[k : k + rows, :]
                    wide_ref[first + i, j] = jnp.where(valid, piece, jnp.zeros_like(piece))
        for ref, first in ((to_a_ref, (1 - lon_odd) * (tile_lon - 2)), (to_b_ref, lon_odd * (tile_lon - 2))):
            collected = []
            for i in range(wide):
                for j in range(2):
                    k = (i * 2 + j) * rows
                    ref[k : k + rows, :] = wide_ref[i, first + j]
                    collected.append(wide_side_ref[i, pl.ds(first + j, 1), :])
            pack_side(ref, count * rows, jnp.concatenate(collected, axis=0))

    vmem = pl.BlockSpec(memory_space=pltpu.VMEM)
    return pl.pallas_call(
        kernel,
        in_specs=[vmem] * 4 + [pl.BlockSpec(memory_space=pl.ANY)],
        out_specs=[vmem] * 4,
        out_shape=[
            jax.ShapeDtypeStruct((wide, tile_lon, rows, members), BF16),
            jax.ShapeDtypeStruct((wide, tile_lon, members), F32),
            jax.ShapeDtypeStruct((payload, members), BF16),
            jax.ShapeDtypeStruct((payload, members), BF16),
        ],
        compiler_params=PARAMS,
        cost_estimate=pl.CostEstimate(flops=10**6, bytes_accessed=3 * 10**6, transcendentals=0),
        name="widen",
    )(q, side, got_a, got_b, after)


def edge_weights(q_ref, side_ref, got_ref, edge, edge_ref, edge_side_ref, store):
    wide, tile_lon, rows, members = q_ref.shape
    tile_lat = wide - 4
    lat = lax.axis_index("lat")
    last = lax.axis_size("lat") - 1
    own, at = edge * (tile_lon - 2), edge * 2
    got_side = unpack_side(got_ref, 2 * wide * rows, 2 * wide)
    for i in range(wide):
        for j in range(2):
            k = (i * 2 + j) * rows
            edge_ref[i, at + j] = got_ref[k : k + rows, :]
            edge_ref[i, 2 - at + j] = q_ref[i, own + j]
        got_part = got_side[2 * i : 2 * i + 2]
        own_part = jnp.where(edge == 0, side_ref[i, :2, :], side_ref[i, tile_lon - 2 :, :])
        edge_side_ref[i, :2, :] = jnp.where(edge == 0, got_part, own_part)
        edge_side_ref[i, 2:, :] = jnp.where(edge == 0, own_part, got_part)
    grams = [row_grams([pair_of(edge_ref, i, 0), pair_of(edge_ref, i, 2)]) for i in range(wide)]
    base = identity(members)
    nodes = [(i, j) for i in range(tile_lat + 2) for j in range(2)]
    sums = [base + 0.5 * (grams[i][j] + grams[i + 2][j]) + grams[i + 1][j] for i, j in nodes]
    sides = [near_side(edge_side_ref, i, j) for i, j in nodes]
    for (i, j), w in zip(nodes, weights_of(sums, sides)):
        if i == 0:
            w = jnp.where(lat == 0, jnp.zeros_like(w), w)
        if i == tile_lat + 1:
            w = jnp.where(lat == last, jnp.zeros_like(w), w)
        store(i, j, w)


def edge_scratch(wide, rows, members):
    return [pltpu.VMEM((wide, 4, rows, members), BF16), pltpu.VMEM((wide, 4, members), F32)]


def near_edge(wide_q, wide_side, got_a):
    wide, tile_lon, rows, members = wide_q.shape

    def kernel(q_ref, side_ref, a_ref, out_ref, edge_ref, edge_side_ref):
        def store(i, j, w):
            out_ref[i, j] = w

        edge = 1 - lax.rem(lax.axis_index("lon"), 2)
        edge_weights(q_ref, side_ref, a_ref, edge, edge_ref, edge_side_ref, store)

    vmem = pl.BlockSpec(memory_space=pltpu.VMEM)
    return pl.pallas_call(
        kernel,
        in_specs=[vmem] * 3,
        out_specs=vmem,
        out_shape=jax.ShapeDtypeStruct((wide - 2, 2, members, members), BF16),
        scratch_shapes=edge_scratch(wide, rows, members),
        compiler_params=PARAMS,
        cost_estimate=pl.CostEstimate(flops=5 * 10**9, bytes_accessed=3 * 10**6, transcendentals=0),
        name="near_edge",
    )(wide_q, wide_side, got_a)


def finish(state, wide_q, wide_side, got_b, inner_w, lat_a_w, lat_b_w, near_w, columns):
    tile_lat, tile_lon, rows, members = state.shape
    wide = tile_lat + 4

    def kernel(
        state_ref, q_ref, side_ref, b_ref, inner_ref, lat_a_ref, lat_b_ref, near_ref, columns_ref,
        out_hbm, edge_ref, edge_side_ref, w_ref, perturb_ref, out_ref, sems,
    ):
        edge = lax.rem(lax.axis_index("lon"), 2)

        def store(i, j, w):
            w_ref[i, edge * tile_lon + j] = w

        edge_weights(q_ref, side_ref, b_ref, edge, edge_ref, edge_side_ref, store)
        for i in range(tile_lat - 2):
            w_ref[2 + i, 2:tile_lon] = inner_ref[i]
        odd = lax.rem(lax.axis_index("lat"), 2)
        for ref, south in ((lat_a_ref, 1 - odd), (lat_b_ref, odd)):
            w_ref[south * (tile_lat + 1), 2:tile_lon] = ref[0]
            w_ref[1 + south * (tile_lat - 1), 2:tile_lon] = ref[1]
        for i in range(tile_lat + 2):
            for j in range(2):
                w_ref[i, (1 - edge) * tile_lon + j] = near_ref[i, j]

        def analyse(i, carry):
            totals = []
            for j in range(tile_lon):
                x = state_ref[i, j].astype(F32)
                mean = jnp.sum(x, axis=1, keepdims=True) * (1.0 / members)
                centred = x - mean
                perturb_ref[j * rows : (j + 1) * rows, :] = centred.astype(BF16)
                totals.append(x - columns_ref[i, 6, j * rows : (j + 1) * rows, :] * centred)
            for n in range(tile_lon + 2):
                low, high = max(n - 2, 0), min(n, tile_lon - 1)
                near = jnp.concatenate([w_ref[i + a, n] for a in range(3)], axis=0)
                out = lax.dot_general(
                    perturb_ref[low * rows : (high + 1) * rows, :],
                    near,
                    (((1,), (1,)), ((), ())),
                    preferred_element_type=F32,
                )
                for j in range(low, high + 1):
                    here = out[(j - low) * rows : (j - low + 1) * rows]
                    span = slice(j * rows, (j + 1) * rows)
                    mixed = 0.0
                    for a in range(3):
                        mixed = mixed + columns_ref[i, a, span, :] * here[:, a * members : (a + 1) * members]
                    totals[j] = totals[j] + columns_ref[i, 3 + n - j, span, :] * mixed
                    if n == j + 2:
                        out_ref[i, j] = totals[j].astype(BF16)
            pltpu.make_async_copy(out_ref.at[i], out_hbm.at[i], sems.at[i]).start()
            return carry

        lax.fori_loop(0, tile_lat, analyse, 0)
        for i in range(tile_lat):
            pltpu.make_async_copy(out_ref.at[i], out_hbm.at[i], sems.at[i]).wait()

    vmem = pl.BlockSpec(memory_space=pltpu.VMEM)
    return pl.pallas_call(
        kernel,
        in_specs=[vmem] * 9,
        out_specs=pl.BlockSpec(memory_space=pltpu.HBM),
        out_shape=jax.ShapeDtypeStruct(state.shape, BF16),
        scratch_shapes=edge_scratch(wide, rows, members)
        + [
            pltpu.VMEM((tile_lat + 2, tile_lon + 2, members, members), BF16),
            pltpu.VMEM((tile_lon * rows, members), BF16),
            pltpu.VMEM(state.shape, BF16),
            pltpu.SemaphoreType.DMA((tile_lat,)),
        ],
        compiler_params=PARAMS,
        cost_estimate=pl.CostEstimate(flops=10**10, bytes_accessed=3 * 10**6, transcendentals=0),
        name="finish",
    )(state, wide_q, wide_side, got_b, inner_w, lat_a_w, lat_b_w, near_w, columns)


def body(state, obs_row, obs_count, obs_value, obs_weight, quadrant, frac_lat, frac_lon, land):
    send_a, side_a = prepare(state, obs_row, obs_count, obs_value, obs_weight)
    got_a = swap(send_a, "lat", 0)
    send_b, q, side, columns, own_grams = complete(
        state, obs_row, obs_count, obs_value, obs_weight, send_a, side_a, quadrant, frac_lat, frac_lon, land
    )
    got_b = swap_inner_lat(send_b)
    inner_w = interior(side, own_grams)
    lat_a_w = lat_edge(0, side, own_grams, got_a)
    wide_q, wide_side, to_a, to_b = widen(q, side, got_a, got_b, lat_a_w)
    lon_b = swap(to_b, "lon", 1)
    lon_a = swap(to_a, "lon", 0)
    lat_b_w = lat_edge(1, side, own_grams, got_b)
    near_w = near_edge(wide_q, wide_side, lon_a)
    return finish(state, wide_q, wide_side, lon_b, inner_w, lat_a_w, lat_b_w, near_w, columns)


def solution(mesh):
    cell = P("lat", "lon", None)
    return jax.shard_map(
        body,
        mesh=mesh,
        in_specs=(
            P("lat", "lon", None, None), cell, P("lat", "lon"), cell, cell, cell, cell, cell, cell,
        ),
        out_specs=P("lat", "lon", None, None),
        check_vma=False,
    )
```

profile of v0, /device:TPU:129, one launch (start us, length us, event | category | flops | bytes accessed | tf_op | source)
XLA Modules:
  0.0 37.6 jit_solution(14597862853605037674)
XLA Ops:
  0.0 2.2 %prepare.1 = (bf16[1056,128]{1,0:T(8,128)(2,1)S(1)}, f32[16,128]{1,0:T(8,128)S(1)}) custom-call(s32[4,8]{1,0:T(4,128)} %refs_0_.3, bf16[4,8,64,128]{3,2,1,0:T(8,128)(2,1)} %state_ref.1, s32[4,8,128]{2,1,0:T(8,128)} %refs_2_.3, f32[4,8,128]{2,1,0:T(8,128)} %refs_3_.3, f32[4,8,128]{2,1,0:T(8,128)} %refs_4_.3), custom_call_target="tpu_custom_call" | custom-call | flops 100000000 | bytes 1000000 | tf_op jit(solution)/shard_map/prepare/pallas_call | solution.py:212
  2.2 1.3 %collective-permute-start = (bf16[1056,128]{1,0:T(8,128)(2,1)S(1)}, bf16[1056,128]{1,0:T(8,128)(2,1)S(1)}, u32[]{:S(2)}, u32[]{:S(2)}) collective-permute-start(bf16[1056,128]{1,0:T(8,128)(2,1)S(1)} %get-tuple-element.16.refs_9_), channel_id=1, source_target_pairs={{0,16},{16,0},{32,48},{48,32},{64,80},{80,64},{96,112},{112,96},{1... | collective-permute-start | bytes 811016 | tf_op jit(solution)/shard_map/ppermute | solution.py:23
  3.5 5.4 %complete.1 = (bf16[1056,128]{1,0:T(8,128)(2,1)S(1)}, bf16[4,8,64,128]{3,2,1,0:T(8,128)(2,1)S(1)}, f32[4,8,128]{2,1,0:T(8,128)S(1)}, f32[4,7,512,128]{3,2,1,0:T(8,128)S(1)}, f32[4,6,128,128]{3,2,1,0:T(8,128)S(1)}) custom-call(s32[4,8]{1,0:T(4,128)} %refs_0_.3, bf16[4,8,64,128]{3,2,1,0:T(8,128)(2,1)} %state_ref.1, s32[4,8,128]{2,1,0:T(8,128)} %refs_2_.3, ...), custom_call_target="tpu_custom_call" | custom-call | flops 1000000000 | bytes 1000000 | tf_op jit(solution)/shard_map/complete/pallas_call | solution.py:300
  8.9 0.1 collective-permute-start.1
  9.0 3.0 %interior.1.inner_ref = bf16[2,6,128,128]{3,2,1,0:T(8,128)(2,1)S(1)} custom-call(f32[4,8,128]{2,1,0:T(8,128)S(1)} %get-tuple-element.19.side_ref, f32[4,6,128,128]{3,2,1,0:T(8,128)S(1)} %get-tuple-element.21.own_ref.gram_ref), custom_call_target="tpu_custom_call" | custom-call | flops 5000000000 | bytes 2000000 | tf_op jit(solution)/shard_map/interior/pallas_call | solution.py:333
  12.1 0.0 collective-permute-done.got_ref.a_ref
  12.1 3.3 %lat_edge.2.after_ref.lat_a_ref = bf16[2,6,128,128]{3,2,1,0:T(8,128)(2,1)S(1)} custom-call(f32[4,8,128]{2,1,0:T(8,128)S(1)} %get-tuple-element.19.side_ref, f32[4,6,128,128]{3,2,1,0:T(8,128)S(1)} %get-tuple-element.21.own_ref.gram_ref, bf16[1056,128]{1,0:T(8,128)(2,1)S(1)} %collective-permute-done.got_ref.a_ref), custom_call_target="tpu_custom_call" | custom-call | flops 5000000000 | bytes 2000000 | tf_op jit(solution)/shard_map/lat_edge/pallas_call | solution.py:380
  15.4 2.7 %collective-permute-done.1.b_ref.got_ref = bf16[1056,128]{1,0:T(8,128)(2,1)S(1)} collective-permute-done((bf16[1056,128]{1,0:T(8,128)(2,1)S(1)}, bf16[1056,128]{1,0:T(8,128)(2,1)S(1)}, u32[]{:S(2)}, u32[]{:S(2)}) %collective-permute-start.1) | collective-permute-done | bytes 270368 | tf_op jit(solution)/shard_map/ppermute | solution.py:35
  18.2 0.2 widen.1
  18.4 3.1 %collective-permute-start.2 = (bf16[1056,128]{1,0:T(8,128)(2,1)S(1)}, bf16[1056,128]{1,0:T(8,128)(2,1)S(1)}, u32[]{:S(2)}, u32[]{:S(2)}) collective-permute-start(bf16[1056,128]{1,0:T(8,128)(2,1)S(1)} %get-tuple-element.24), channel_id=1, source_target_pairs={{1,2},{2,1},{3,4},{4,3},{5,6},{6,5},{7,8},{8,7},{9,10},{10,9},{11,... | collective-permute-start | bytes 811016 | tf_op jit(solution)/shard_map/ppermute | solution.py:23
  21.5 2.3 %collective-permute-start.3 = (bf16[1056,128]{1,0:T(8,128)(2,1)S(1)}, bf16[1056,128]{1,0:T(8,128)(2,1)S(1)}, u32[]{:S(2)}, u32[]{:S(2)}) collective-permute-start(bf16[1056,128]{1,0:T(8,128)(2,1)S(1)} %get-tuple-element.25), channel_id=1, source_target_pairs={{0,1},{1,0},{2,3},{3,2},{4,5},{5,4},{6,7},{7,6},{8,9},{9,8},{10,11... | collective-permute-start | bytes 811016 | tf_op jit(solution)/shard_map/ppermute | solution.py:23
  23.7 3.3 %lat_edge.3.lat_b_ref = bf16[2,6,128,128]{3,2,1,0:T(8,128)(2,1)S(1)} custom-call(f32[4,8,128]{2,1,0:T(8,128)S(1)} %get-tuple-element.19.side_ref, f32[4,6,128,128]{3,2,1,0:T(8,128)S(1)} %get-tuple-element.21.own_ref.gram_ref, bf16[1056,128]{1,0:T(8,128)(2,1)S(1)} %collective-permute-done.1.b_ref.got_ref), custom_call_target="tpu_custom_call" | custom-call | flops 5000000000 | bytes 2000000 | tf_op jit(solution)/shard_map/lat_edge/pallas_call | solution.py:380
  27.1 0.0 collective-permute-done.3.a_ref
  27.1 0.0 copy-start
  27.1 3.5 %near_edge.1.near_ref = bf16[6,2,128,128]{3,2,1,0:T(8,128)(2,1)S(1)} custom-call(bf16[8,8,64,128]{3,2,1,0:T(8,128)(2,1)S(1)} %get-tuple-element.22.q_ref, f32[8,8,128]{2,1,0:T(8,128)S(1)} %get-tuple-element.23.side_ref, bf16[1056,128]{1,0:T(8,128)(2,1)S(1)} %collective-permute-done.3.a_ref), custom_call_target="tpu_custom_call" | custom-call | flops 5000000000 | bytes 3000000 | tf_op jit(solution)/shard_map/near_edge/pallas_call | solution.py:492
  30.6 0.0 collective-permute-done.2.b_ref
  30.6 0.0 copy-done
  30.6 6.9 %finish.1 = bf16[4,8,64,128]{3,2,1,0:T(8,128)(2,1)} custom-call(bf16[4,8,64,128]{3,2,1,0:T(8,128)(2,1)S(1)} %copy-done, bf16[8,8,64,128]{3,2,1,0:T(8,128)(2,1)S(1)} %get-tuple-element.22.q_ref, f32[8,8,128]{2,1,0:T(8,128)S(1)} %get-tuple-element.23.side_ref, bf16[1056,128]{1,0:T(8,128)(2,1)S(1)} %collective-permute-done.2.b_ref, ...), custom_call_target="tpu_custom_call" | custom-call | flops 10000000000 | bytes 3000000 | tf_op jit(solution)/shard_map/finish/pallas_call | solution.py:562
Async XLA Ops:
  2.2 9.9 %collective-permute-start = (bf16[1056,128]{1,0:T(8,128)(2,1)S(1)}, bf16[1056,128]{1,0:T(8,128)(2,1)S(1)}, u32[]{:S(2)}, u32[]{:S(2)}) collective-permute-start(bf16[1056,128]{1,0:T(8,128)(2,1)S(1)} %get-tuple-element.16.refs_9_), channel_id=1, source_target_pairs={{0,16},{16,0},{32,48},{48,32},{64,80},{80,64},{96,112},{112,96},{1... | collective-permute-start | bytes 811016 | tf_op jit(solution)/shard_map/ppermute | solution.py:23
  8.9 9.2 %collective-permute-start.1 = (bf16[1056,128]{1,0:T(8,128)(2,1)S(1)}, bf16[1056,128]{1,0:T(8,128)(2,1)S(1)}, u32[]{:S(2)}, u32[]{:S(2)}) collective-permute-start(bf16[1056,128]{1,0:T(8,128)(2,1)S(1)} %get-tuple-element.20), channel_id=1, source_target_pairs={{16,32},{32,16},{48,64},{64,48},{80,96},{96,80},{112,128},{128,112... | collective-permute-start | bytes 811016 | tf_op jit(solution)/shard_map/ppermute | solution.py:35
  18.4 12.2 %collective-permute-start.2 = (bf16[1056,128]{1,0:T(8,128)(2,1)S(1)}, bf16[1056,128]{1,0:T(8,128)(2,1)S(1)}, u32[]{:S(2)}, u32[]{:S(2)}) collective-permute-start(bf16[1056,128]{1,0:T(8,128)(2,1)S(1)} %get-tuple-element.24), channel_id=1, source_target_pairs={{1,2},{2,1},{3,4},{4,3},{5,6},{6,5},{7,8},{8,7},{9,10},{10,9},{11,... | collective-permute-start | bytes 811016 | tf_op jit(solution)/shard_map/ppermute | solution.py:23
  21.5 5.6 %collective-permute-start.3 = (bf16[1056,128]{1,0:T(8,128)(2,1)S(1)}, bf16[1056,128]{1,0:T(8,128)(2,1)S(1)}, u32[]{:S(2)}, u32[]{:S(2)}) collective-permute-start(bf16[1056,128]{1,0:T(8,128)(2,1)S(1)} %get-tuple-element.25), channel_id=1, source_target_pairs={{0,1},{1,0},{2,3},{3,2},{4,5},{5,4},{6,7},{7,6},{8,9},{9,8},{10,11... | collective-permute-start | bytes 811016 | tf_op jit(solution)/shard_map/ppermute | solution.py:23
  27.1 3.5 %copy-start = (bf16[4,8,64,128]{3,2,1,0:T(8,128)(2,1)S(1)}, bf16[4,8,64,128]{3,2,1,0:T(8,128)(2,1)}, u32[]{:S(2)}) copy-start(bf16[4,8,64,128]{3,2,1,0:T(8,128)(2,1)} %state_ref.1) | copy-start | bytes 1572868
where the time goes:
time: 37.7 us; the launch traced here: 37.6 us
  Pallas kernels  27.8 us (74%)
  starting transfers between devices  6.78 us (18%)
  waiting for transfers between devices  2.75 us (7%)
    pallas_call x1, Pallas kernels, finish(): pl.pallas_call(kernel, in_specs=[vmem] * 9, out_specs=pl.BlockSpec(memory...  6.86 us
    ppermute x3, starting transfers between devices, swap(): return lax.ppermute(x, axis, pairs)  6.69 us
    pallas_call x2, Pallas kernels, lat_edge(): pl.pallas_call(kernel, in_specs=[vmem] * 3, out_specs=vmem, out_shape=jax...  6.66 us
    pallas_call x1, Pallas kernels, complete(): pl.pallas_call(kernel, in_specs=[pl.BlockSpec(memory_space=pltpu.HBM)] *...  5.42 us
    pallas_call x1, Pallas kernels, near_edge(): pl.pallas_call(kernel, in_specs=[vmem] * 3, out_specs=vmem, out_shape=jax...  3.47 us
    pallas_call x1, Pallas kernels, interior(): pl.pallas_call(kernel, in_specs=[vmem] * 2, out_specs=vmem, out_shape=jax...  3.02 us
    ppermute x1, waiting for transfers between devices, swap_inner_lat(): return lax.ppermute(x, ('lat', 'lon'), pairs)  2.74 us
    pallas_call x1, Pallas kernels, prepare(): pl.pallas_call(kernel, in_specs=[pl.BlockSpec(memory_space=pltpu.HBM)] *...  2.19 us
  transfers between devices with their start and end apart: 4, of which 1 were waited for; matrix products, arithmetic and copies ran while one was open for 0% of the time, Pallas kernels for 49%

commit v1 on v0

--- a/solution.py
+++ b/solution.py
@@ -260,15 +260,10 @@
                     gram_ref[first + i, j] = gram
 
         place(a_ref, a_side_ref, a_first)
-        for copy in copies:
-            copy.wait()
-        cell_rows(b_first, cells, b_ref, b_side_ref)
-        place(b_ref, b_side_ref, b_first)
         coef_ref[...] = jnp.zeros_like(coef_ref)
         for copy in placing_copies:
             copy.wait()
-
-        def columns(i, carry):
+        for i in range(tile_lat):
             quad = quad_ref[i]
             fa, fo = flat_ref[i], flon_ref[i]
             dry = jnp.where(land_ref[i] == 1, F32(1.0), F32(0.0))
@@ -276,25 +271,24 @@
             zero = jnp.zeros_like(fa)
             coefs = (
                 jnp.where(north, 1.0 - fa, zero) * dry,
-                jnp.where(north, fa, 1.0 - fa) * dry,
                 jnp.where(north, zero, fa) * dry,
                 jnp.where(west, 1.0 - fo, zero),
-                jnp.where(west, fo, 1.0 - fo),
                 jnp.where(west, zero, fo),
                 dry,
             )
             for k, coef in enumerate(coefs):
-                coef_ref[k * tile_lon : (k + 1) * tile_lon, :rows] = coef
-            turned = coef_ref[...].T
+                coef_ref[i, k * tile_lon : (k + 1) * tile_lon, :rows] = coef
+            turned = coef_ref[i].T
             for k in range(len(coefs)):
                 for j in range(tile_lon):
                     at = k * tile_lon + j
                     columns_ref[i, k, j * rows : (j + 1) * rows, :] = jnp.broadcast_to(
                         turned[:rows, at : at + 1], (rows, members)
                     )
-            return carry
-
-        lax.fori_loop(0, tile_lat, columns, 0)
+        for copy in copies:
+            copy.wait()
+        cell_rows(b_first, cells, b_ref, b_side_ref)
+        place(b_ref, b_side_ref, b_first)
 
     vmem = pl.BlockSpec(memory_space=pltpu.VMEM)
     return pl.pallas_call(
@@ -305,11 +299,11 @@
             jax.ShapeDtypeStruct(first_rows.shape, BF16),
             jax.ShapeDtypeStruct(state.shape, BF16),
             jax.ShapeDtypeStruct((tile_lat, tile_lon, members), F32),
-            jax.ShapeDtypeStruct((tile_lat, 7, tile_lon * rows, members), F32),
+            jax.ShapeDtypeStruct((tile_lat, 5, tile_lon * rows, members), F32),
             jax.ShapeDtypeStruct((tile_lat, tile_lon - 2, members, members), F32),
         ],
         scratch_shapes=cell_scratch(*arrays)
-        + [pltpu.VMEM((half, members), F32), pltpu.VMEM((128, 128), F32)]
+        + [pltpu.VMEM((half, members), F32), pltpu.VMEM((tile_lat, 128, 128), F32)]
         + [pltpu.VMEM(x.shape, x.dtype) for x in placing]
         + [pltpu.SemaphoreType.DMA((4,))],
         compiler_params=PARAMS,
@@ -532,7 +526,7 @@
                 mean = jnp.sum(x, axis=1, keepdims=True) * (1.0 / members)
                 centred = x - mean
                 perturb_ref[j * rows : (j + 1) * rows, :] = centred.astype(BF16)
-                totals.append(x - columns_ref[i, 6, j * rows : (j + 1) * rows, :] * centred)
+                totals.append(x - columns_ref[i, 4, j * rows : (j + 1) * rows, :] * centred)
             for n in range(tile_lon + 2):
                 low, high = max(n - 2, 0), min(n, tile_lon - 1)
                 near = jnp.concatenate([w_ref[i + a, n] for a in range(3)], axis=0)
@@ -545,10 +539,16 @@
                 for j in range(low, high + 1):
                     here = out[(j - low) * rows : (j - low + 1) * rows]
                     span = slice(j * rows, (j + 1) * rows)
+                    first, third = columns_ref[i, 0, span, :], columns_ref[i, 1, span, :]
+                    along = (first, columns_ref[i, 4, span, :] - first - third, third)
                     mixed = 0.0
                     for a in range(3):
-                        mixed = mixed + columns_ref[i, a, span, :] * here[:, a * members : (a + 1) * members]
-                    totals[j] = totals[j] + columns_ref[i, 3 + n - j, span, :] * mixed
+                        mixed = mixed + along[a] * here[:, a * members : (a + 1) * members]
+                    if n - j == 1:
+                        across = 1.0 - columns_ref[i, 2, span, :] - columns_ref[i, 3, span, :]
+                    else:
+                        across = columns_ref[i, 2 + (n - j) // 2, span, :]
+                    totals[j] = totals[j] + across * mixed
                     if n == j + 2:
                         out_ref[i, j] = totals[j].astype(BF16)
             pltpu.make_async_copy(out_ref.at[i], out_hbm.at[i], sems.at[i]).start()

time: 37.7 us -> 36.6 us (0.971)
  Pallas kernels: 27.8 us -> 26.5 us
    pallas_call x1, Pallas kernels: 5.42 us -> 4.09 us  [complete(): pl.pallas_call(kernel, in_specs=[pl.BlockSpec(memory_space=pltpu.HBM)] *...]
  transfers between devices with their start and end apart: 4 -> 4, of which waited for: 1 -> 1; matrix products, arithmetic and copies ran while one was open for 0% -> 0% of each run, Pallas kernels for 49% -> 47%
where the time goes in v1:
time: 36.6 us; the launch traced here: 36.3 us
  Pallas kernels  26.5 us (72%)
  starting transfers between devices  6.78 us (19%)
  waiting for transfers between devices  2.75 us (8%)
    pallas_call x1, Pallas kernels, finish(): pl.pallas_call(kernel, in_specs=[vmem] * 9, out_specs=pl.BlockSpec(memory...  6.83 us
    ppermute x3, starting transfers between devices, swap(): return lax.ppermute(x, axis, pairs)  6.69 us
    pallas_call x2, Pallas kernels, lat_edge(): pl.pallas_call(kernel, in_specs=[vmem] * 3, out_specs=vmem, out_shape=jax...  6.66 us
    pallas_call x1, Pallas kernels, complete(): pl.pallas_call(kernel, in_specs=[pl.BlockSpec(memory_space=pltpu.HBM)] *...  4.09 us
    pallas_call x1, Pallas kernels, near_edge(): pl.pallas_call(kernel, in_specs=[vmem] * 3, out_specs=vmem, out_shape=jax...  3.47 us
    pallas_call x1, Pallas kernels, interior(): pl.pallas_call(kernel, in_specs=[vmem] * 2, out_specs=vmem, out_shape=jax...  3.02 us
    ppermute x1, waiting for transfers between devices, swap_inner_lat(): return lax.ppermute(x, ('lat', 'lon'), pairs)  2.74 us
    pallas_call x1, Pallas kernels, prepare(): pl.pallas_call(kernel, in_specs=[pl.BlockSpec(memory_space=pltpu.HBM)] *...  2.19 us
  transfers between devices with their start and end apart: 4, of which 1 were waited for; matrix products, arithmetic and copies ran while one was open for 0% of the time, Pallas kernels for 47%

profile of v1, /device:TPU:129, one launch (start us, length us, event | category | flops | bytes accessed | tf_op | source)
XLA Modules:
  0.0 36.3 jit_solution(6792504963677677718)
XLA Ops:
  0.0 2.2 %prepare.1 = (bf16[1056,128]{1,0:T(8,128)(2,1)S(1)}, f32[16,128]{1,0:T(8,128)S(1)}) custom-call(s32[4,8]{1,0:T(4,128)} %refs_0_.3, bf16[4,8,64,128]{3,2,1,0:T(8,128)(2,1)} %state_ref.1, s32[4,8,128]{2,1,0:T(8,128)} %refs_2_.3, f32[4,8,128]{2,1,0:T(8,128)} %refs_3_.3, f32[4,8,128]{2,1,0:T(8,128)} %refs_4_.3), custom_call_target="tpu_custom_call" | custom-call | flops 100000000 | bytes 1000000 | tf_op jit(solution)/shard_map/prepare/pallas_call | solution.py:212
  2.2 1.3 %collective-permute-start = (bf16[1056,128]{1,0:T(8,128)(2,1)S(1)}, bf16[1056,128]{1,0:T(8,128)(2,1)S(1)}, u32[]{:S(2)}, u32[]{:S(2)}) collective-permute-start(bf16[1056,128]{1,0:T(8,128)(2,1)S(1)} %get-tuple-element.16.refs_9_), channel_id=1, source_target_pairs={{0,16},{16,0},{32,48},{48,32},{64,80},{80,64},{96,112},{112,96},{1... | collective-permute-start | bytes 811016 | tf_op jit(solution)/shard_map/ppermute | solution.py:23
  3.5 4.1 %complete.1 = (bf16[1056,128]{1,0:T(8,128)(2,1)S(1)}, bf16[4,8,64,128]{3,2,1,0:T(8,128)(2,1)S(1)}, f32[4,8,128]{2,1,0:T(8,128)S(1)}, f32[4,5,512,128]{3,2,1,0:T(8,128)S(1)}, f32[4,6,128,128]{3,2,1,0:T(8,128)S(1)}) custom-call(s32[4,8]{1,0:T(4,128)} %refs_0_.3, bf16[4,8,64,128]{3,2,1,0:T(8,128)(2,1)} %state_ref.1, s32[4,8,128]{2,1,0:T(8,128)} %refs_2_.3, ...), custom_call_target="tpu_custom_call" | custom-call | flops 1000000000 | bytes 1000000 | tf_op jit(solution)/shard_map/complete/pallas_call | solution.py:294
  7.6 0.1 collective-permute-start.1
  7.7 3.0 %interior.1.inner_ref = bf16[2,6,128,128]{3,2,1,0:T(8,128)(2,1)S(1)} custom-call(f32[4,8,128]{2,1,0:T(8,128)S(1)} %get-tuple-element.19.side_ref, f32[4,6,128,128]{3,2,1,0:T(8,128)S(1)} %get-tuple-element.21.own_ref.gram_ref), custom_call_target="tpu_custom_call" | custom-call | flops 5000000000 | bytes 2000000 | tf_op jit(solution)/shard_map/interior/pallas_call | solution.py:327
  10.7 0.0 collective-permute-done.got_ref.a_ref
  10.7 3.3 %lat_edge.2.after_ref.lat_a_ref = bf16[2,6,128,128]{3,2,1,0:T(8,128)(2,1)S(1)} custom-call(f32[4,8,128]{2,1,0:T(8,128)S(1)} %get-tuple-element.19.side_ref, f32[4,6,128,128]{3,2,1,0:T(8,128)S(1)} %get-tuple-element.21.own_ref.gram_ref, bf16[1056,128]{1,0:T(8,128)(2,1)S(1)} %collective-permute-done.got_ref.a_ref), custom_call_target="tpu_custom_call" | custom-call | flops 5000000000 | bytes 2000000 | tf_op jit(solution)/shard_map/lat_edge/pallas_call | solution.py:374
  14.1 2.7 %collective-permute-done.1.b_ref.got_ref = bf16[1056,128]{1,0:T(8,128)(2,1)S(1)} collective-permute-done((bf16[1056,128]{1,0:T(8,128)(2,1)S(1)}, bf16[1056,128]{1,0:T(8,128)(2,1)S(1)}, u32[]{:S(2)}, u32[]{:S(2)}) %collective-permute-start.1) | collective-permute-done | bytes 270368 | tf_op jit(solution)/shard_map/ppermute | solution.py:35
  16.8 0.2 widen.1
  17.0 3.8 %collective-permute-start.2 = (bf16[1056,128]{1,0:T(8,128)(2,1)S(1)}, bf16[1056,128]{1,0:T(8,128)(2,1)S(1)}, u32[]{:S(2)}, u32[]{:S(2)}) collective-permute-start(bf16[1056,128]{1,0:T(8,128)(2,1)S(1)} %get-tuple-element.24), channel_id=1, source_target_pairs={{1,2},{2,1},{3,4},{4,3},{5,6},{6,5},{7,8},{8,7},{9,10},{10,9},{11,... | collective-permute-start | bytes 811016 | tf_op jit(solution)/shard_map/ppermute | solution.py:23
  20.8 1.6 %collective-permute-start.3 = (bf16[1056,128]{1,0:T(8,128)(2,1)S(1)}, bf16[1056,128]{1,0:T(8,128)(2,1)S(1)}, u32[]{:S(2)}, u32[]{:S(2)}) collective-permute-start(bf16[1056,128]{1,0:T(8,128)(2,1)S(1)} %get-tuple-element.25), channel_id=1, source_target_pairs={{0,1},{1,0},{2,3},{3,2},{4,5},{5,4},{6,7},{7,6},{8,9},{9,8},{10,11... | collective-permute-start | bytes 811016 | tf_op jit(solution)/shard_map/ppermute | solution.py:23
  22.4 3.3 %lat_edge.3.lat_b_ref = bf16[2,6,128,128]{3,2,1,0:T(8,128)(2,1)S(1)} custom-call(f32[4,8,128]{2,1,0:T(8,128)S(1)} %get-tuple-element.19.side_ref, f32[4,6,128,128]{3,2,1,0:T(8,128)S(1)} %get-tuple-element.21.own_ref.gram_ref, bf16[1056,128]{1,0:T(8,128)(2,1)S(1)} %collective-permute-done.1.b_ref.got_ref), custom_call_target="tpu_custom_call" | custom-call | flops 5000000000 | bytes 2000000 | tf_op jit(solution)/shard_map/lat_edge/pallas_call | solution.py:374
  25.7 0.0 collective-permute-done.3.a_ref
  25.8 0.0 copy-start
  25.8 3.5 %near_edge.1.near_ref = bf16[6,2,128,128]{3,2,1,0:T(8,128)(2,1)S(1)} custom-call(bf16[8,8,64,128]{3,2,1,0:T(8,128)(2,1)S(1)} %get-tuple-element.22.q_ref, f32[8,8,128]{2,1,0:T(8,128)S(1)} %get-tuple-element.23.side_ref, bf16[1056,128]{1,0:T(8,128)(2,1)S(1)} %collective-permute-done.3.a_ref), custom_call_target="tpu_custom_call" | custom-call | flops 5000000000 | bytes 3000000 | tf_op jit(solution)/shard_map/near_edge/pallas_call | solution.py:486
  29.2 0.0 collective-permute-done.2.b_ref
  29.3 0.0 copy-done
  29.3 6.8 %finish.1 = bf16[4,8,64,128]{3,2,1,0:T(8,128)(2,1)} custom-call(bf16[4,8,64,128]{3,2,1,0:T(8,128)(2,1)S(1)} %copy-done, bf16[8,8,64,128]{3,2,1,0:T(8,128)(2,1)S(1)} %get-tuple-element.22.q_ref, f32[8,8,128]{2,1,0:T(8,128)S(1)} %get-tuple-element.23.side_ref, bf16[1056,128]{1,0:T(8,128)(2,1)S(1)} %collective-permute-done.2.b_ref, ...), custom_call_target="tpu_custom_call" | custom-call | flops 10000000000 | bytes 3000000 | tf_op jit(solution)/shard_map/finish/pallas_call | solution.py:562
Async XLA Ops:
  2.2 8.5 %collective-permute-start = (bf16[1056,128]{1,0:T(8,128)(2,1)S(1)}, bf16[1056,128]{1,0:T(8,128)(2,1)S(1)}, u32[]{:S(2)}, u32[]{:S(2)}) collective-permute-start(bf16[1056,128]{1,0:T(8,128)(2,1)S(1)} %get-tuple-element.16.refs_9_), channel_id=1, source_target_pairs={{0,16},{16,0},{32,48},{48,32},{64,80},{80,64},{96,112},{112,96},{1... | collective-permute-start | bytes 811016 | tf_op jit(solution)/shard_map/ppermute | solution.py:23
  7.6 9.2 %collective-permute-start.1 = (bf16[1056,128]{1,0:T(8,128)(2,1)S(1)}, bf16[1056,128]{1,0:T(8,128)(2,1)S(1)}, u32[]{:S(2)}, u32[]{:S(2)}) collective-permute-start(bf16[1056,128]{1,0:T(8,128)(2,1)S(1)} %get-tuple-element.20), channel_id=1, source_target_pairs={{16,32},{32,16},{48,64},{64,48},{80,96},{96,80},{112,128},{128,112... | collective-permute-start | bytes 811016 | tf_op jit(solution)/shard_map/ppermute | solution.py:35
  17.0 12.2 %collective-permute-start.2 = (bf16[1056,128]{1,0:T(8,128)(2,1)S(1)}, bf16[1056,128]{1,0:T(8,128)(2,1)S(1)}, u32[]{:S(2)}, u32[]{:S(2)}) collective-permute-start(bf16[1056,128]{1,0:T(8,128)(2,1)S(1)} %get-tuple-element.24), channel_id=1, source_target_pairs={{1,2},{2,1},{3,4},{4,3},{5,6},{6,5},{7,8},{8,7},{9,10},{10,9},{11,... | collective-permute-start | bytes 811016 | tf_op jit(solution)/shard_map/ppermute | solution.py:23
  20.8 4.9 %collective-permute-start.3 = (bf16[1056,128]{1,0:T(8,128)(2,1)S(1)}, bf16[1056,128]{1,0:T(8,128)(2,1)S(1)}, u32[]{:S(2)}, u32[]{:S(2)}) collective-permute-start(bf16[1056,128]{1,0:T(8,128)(2,1)S(1)} %get-tuple-element.25), channel_id=1, source_target_pairs={{0,1},{1,0},{2,3},{3,2},{4,5},{5,4},{6,7},{7,6},{8,9},{9,8},{10,11... | collective-permute-start | bytes 811016 | tf_op jit(solution)/shard_map/ppermute | solution.py:23
  25.8 3.5 %copy-start = (bf16[4,8,64,128]{3,2,1,0:T(8,128)(2,1)S(1)}, bf16[4,8,64,128]{3,2,1,0:T(8,128)(2,1)}, u32[]{:S(2)}) copy-start(bf16[4,8,64,128]{3,2,1,0:T(8,128)(2,1)} %state_ref.1) | copy-start | bytes 1572868

commit v2 on v1

--- a/solution.py
+++ b/solution.py
@@ -554,7 +554,7 @@
             pltpu.make_async_copy(out_ref.at[i], out_hbm.at[i], sems.at[i]).start()
             return carry
 
-        lax.fori_loop(0, tile_lat, analyse, 0)
+        lax.fori_loop(0, tile_lat, analyse, 0, unroll=True)
         for i in range(tile_lat):
             pltpu.make_async_copy(out_ref.at[i], out_hbm.at[i], sems.at[i]).wait()
 

time: 36.6 us -> 36.1 us (0.986)
  Pallas kernels: 26.5 us -> 26 us
    pallas_call x1, Pallas kernels: 6.83 us -> 6.32 us  [finish(): pl.pallas_call(kernel, in_specs=[vmem] * 9, out_specs=pl.BlockSpec(memory...]
  transfers between devices with their start and end apart: 4 -> 4, of which waited for: 1 -> 1; matrix products, arithmetic and copies ran while one was open for 0% -> 0% of each run, Pallas kernels for 47% -> 48%
where the time goes in v2:
time: 36.1 us; the launch traced here: 35.7 us
  Pallas kernels  26 us (72%)
  starting transfers between devices  6.78 us (19%)
  waiting for transfers between devices  2.75 us (8%)
    ppermute x3, starting transfers between devices, swap(): return lax.ppermute(x, axis, pairs)  6.69 us
    pallas_call x2, Pallas kernels, lat_edge(): pl.pallas_call(kernel, in_specs=[vmem] * 3, out_specs=vmem, out_shape=jax...  6.66 us
    pallas_call x1, Pallas kernels, finish(): pl.pallas_call(kernel, in_specs=[vmem] * 9, out_specs=pl.BlockSpec(memory...  6.32 us
    pallas_call x1, Pallas kernels, complete(): pl.pallas_call(kernel, in_specs=[pl.BlockSpec(memory_space=pltpu.HBM)] *...  4.09 us
    pallas_call x1, Pallas kernels, near_edge(): pl.pallas_call(kernel, in_specs=[vmem] * 3, out_specs=vmem, out_shape=jax...  3.47 us
    pallas_call x1, Pallas kernels, interior(): pl.pallas_call(kernel, in_specs=[vmem] * 2, out_specs=vmem, out_shape=jax...  3.02 us
    ppermute x1, waiting for transfers between devices, swap_inner_lat(): return lax.ppermute(x, ('lat', 'lon'), pairs)  2.74 us
    pallas_call x1, Pallas kernels, prepare(): pl.pallas_call(kernel, in_specs=[pl.BlockSpec(memory_space=pltpu.HBM)] *...  2.19 us
  transfers between devices with their start and end apart: 4, of which 1 were waited for; matrix products, arithmetic and copies ran while one was open for 0% of the time, Pallas kernels for 48%

profile of v2, /device:TPU:129, one launch (start us, length us, event | category | flops | bytes accessed | tf_op | source)
XLA Modules:
  0.0 35.7 jit_solution(4256130326554625757)
XLA Ops:
  0.0 2.2 %prepare.1 = (bf16[1056,128]{1,0:T(8,128)(2,1)S(1)}, f32[16,128]{1,0:T(8,128)S(1)}) custom-call(s32[4,8]{1,0:T(4,128)} %refs_0_.3, bf16[4,8,64,128]{3,2,1,0:T(8,128)(2,1)} %state_ref.1, s32[4,8,128]{2,1,0:T(8,128)} %refs_2_.3, f32[4,8,128]{2,1,0:T(8,128)} %refs_3_.3, f32[4,8,128]{2,1,0:T(8,128)} %refs_4_.3), custom_call_target="tpu_custom_call" | custom-call | flops 100000000 | bytes 1000000 | tf_op jit(solution)/shard_map/prepare/pallas_call | solution.py:212
  2.2 1.3 %collective-permute-start = (bf16[1056,128]{1,0:T(8,128)(2,1)S(1)}, bf16[1056,128]{1,0:T(8,128)(2,1)S(1)}, u32[]{:S(2)}, u32[]{:S(2)}) collective-permute-start(bf16[1056,128]{1,0:T(8,128)(2,1)S(1)} %get-tuple-element.16.refs_9_), channel_id=1, source_target_pairs={{0,16},{16,0},{32,48},{48,32},{64,80},{80,64},{96,112},{112,96},{1... | collective-permute-start | bytes 811016 | tf_op jit(solution)/shard_map/ppermute | solution.py:23
  3.5 4.1 %complete.1 = (bf16[1056,128]{1,0:T(8,128)(2,1)S(1)}, bf16[4,8,64,128]{3,2,1,0:T(8,128)(2,1)S(1)}, f32[4,8,128]{2,1,0:T(8,128)S(1)}, f32[4,5,512,128]{3,2,1,0:T(8,128)S(1)}, f32[4,6,128,128]{3,2,1,0:T(8,128)S(1)}) custom-call(s32[4,8]{1,0:T(4,128)} %refs_0_.3, bf16[4,8,64,128]{3,2,1,0:T(8,128)(2,1)} %state_ref.1, s32[4,8,128]{2,1,0:T(8,128)} %refs_2_.3, ...), custom_call_target="tpu_custom_call" | custom-call | flops 1000000000 | bytes 1000000 | tf_op jit(solution)/shard_map/complete/pallas_call | solution.py:294
  7.6 0.1 collective-permute-start.1
  7.7 3.0 %interior.1.inner_ref = bf16[2,6,128,128]{3,2,1,0:T(8,128)(2,1)S(1)} custom-call(f32[4,8,128]{2,1,0:T(8,128)S(1)} %get-tuple-element.19.side_ref, f32[4,6,128,128]{3,2,1,0:T(8,128)S(1)} %get-tuple-element.21.own_ref.gram_ref), custom_call_target="tpu_custom_call" | custom-call | flops 5000000000 | bytes 2000000 | tf_op jit(solution)/shard_map/interior/pallas_call | solution.py:327
  10.7 0.0 collective-permute-done.got_ref.a_ref
  10.7 3.3 %lat_edge.2.after_ref.lat_a_ref = bf16[2,6,128,128]{3,2,1,0:T(8,128)(2,1)S(1)} custom-call(f32[4,8,128]{2,1,0:T(8,128)S(1)} %get-tuple-element.19.side_ref, f32[4,6,128,128]{3,2,1,0:T(8,128)S(1)} %get-tuple-element.21.own_ref.gram_ref, bf16[1056,128]{1,0:T(8,128)(2,1)S(1)} %collective-permute-done.got_ref.a_ref), custom_call_target="tpu_custom_call" | custom-call | flops 5000000000 | bytes 2000000 | tf_op jit(solution)/shard_map/lat_edge/pallas_call | solution.py:374
  14.1 2.7 %collective-permute-done.1.b_ref.got_ref = bf16[1056,128]{1,0:T(8,128)(2,1)S(1)} collective-permute-done((bf16[1056,128]{1,0:T(8,128)(2,1)S(1)}, bf16[1056,128]{1,0:T(8,128)(2,1)S(1)}, u32[]{:S(2)}, u32[]{:S(2)}) %collective-permute-start.1) | collective-permute-done | bytes 270368 | tf_op jit(solution)/shard_map/ppermute | solution.py:35
  16.8 0.2 widen.1
  17.0 3.8 %collective-permute-start.2 = (bf16[1056,128]{1,0:T(8,128)(2,1)S(1)}, bf16[1056,128]{1,0:T(8,128)(2,1)S(1)}, u32[]{:S(2)}, u32[]{:S(2)}) collective-permute-start(bf16[1056,128]{1,0:T(8,128)(2,1)S(1)} %get-tuple-element.24), channel_id=1, source_target_pairs={{1,2},{2,1},{3,4},{4,3},{5,6},{6,5},{7,8},{8,7},{9,10},{10,9},{11,... | collective-permute-start | bytes 811016 | tf_op jit(solution)/shard_map/ppermute | solution.py:23
  20.8 1.6 %collective-permute-start.3 = (bf16[1056,128]{1,0:T(8,128)(2,1)S(1)}, bf16[1056,128]{1,0:T(8,128)(2,1)S(1)}, u32[]{:S(2)}, u32[]{:S(2)}) collective-permute-start(bf16[1056,128]{1,0:T(8,128)(2,1)S(1)} %get-tuple-element.25), channel_id=1, source_target_pairs={{0,1},{1,0},{2,3},{3,2},{4,5},{5,4},{6,7},{7,6},{8,9},{9,8},{10,11... | collective-permute-start | bytes 811016 | tf_op jit(solution)/shard_map/ppermute | solution.py:23
  22.4 3.3 %lat_edge.3.lat_b_ref = bf16[2,6,128,128]{3,2,1,0:T(8,128)(2,1)S(1)} custom-call(f32[4,8,128]{2,1,0:T(8,128)S(1)} %get-tuple-element.19.side_ref, f32[4,6,128,128]{3,2,1,0:T(8,128)S(1)} %get-tuple-element.21.own_ref.gram_ref, bf16[1056,128]{1,0:T(8,128)(2,1)S(1)} %collective-permute-done.1.b_ref.got_ref), custom_call_target="tpu_custom_call" | custom-call | flops 5000000000 | bytes 2000000 | tf_op jit(solution)/shard_map/lat_edge/pallas_call | solution.py:374
  25.7 0.0 collective-permute-done.3.a_ref
  25.8 0.0 copy-start
  25.8 3.5 %near_edge.1.near_ref = bf16[6,2,128,128]{3,2,1,0:T(8,128)(2,1)S(1)} custom-call(bf16[8,8,64,128]{3,2,1,0:T(8,128)(2,1)S(1)} %get-tuple-element.22.q_ref, f32[8,8,128]{2,1,0:T(8,128)S(1)} %get-tuple-element.23.side_ref, bf16[1056,128]{1,0:T(8,128)(2,1)S(1)} %collective-permute-done.3.a_ref), custom_call_target="tpu_custom_call" | custom-call | flops 5000000000 | bytes 3000000 | tf_op jit(solution)/shard_map/near_edge/pallas_call | solution.py:486
  29.2 0.0 collective-permute-done.2.b_ref
  29.3 0.0 copy-done
  29.3 6.3 %finish.1 = bf16[4,8,64,128]{3,2,1,0:T(8,128)(2,1)} custom-call(bf16[4,8,64,128]{3,2,1,0:T(8,128)(2,1)S(1)} %copy-done, bf16[8,8,64,128]{3,2,1,0:T(8,128)(2,1)S(1)} %get-tuple-element.22.q_ref, f32[8,8,128]{2,1,0:T(8,128)S(1)} %get-tuple-element.23.side_ref, bf16[1056,128]{1,0:T(8,128)(2,1)S(1)} %collective-permute-done.2.b_ref, ...), custom_call_target="tpu_custom_call" | custom-call | flops 10000000000 | bytes 3000000 | tf_op jit(solution)/shard_map/finish/pallas_call | solution.py:562
Async XLA Ops:
  2.2 8.5 %collective-permute-start = (bf16[1056,128]{1,0:T(8,128)(2,1)S(1)}, bf16[1056,128]{1,0:T(8,128)(2,1)S(1)}, u32[]{:S(2)}, u32[]{:S(2)}) collective-permute-start(bf16[1056,128]{1,0:T(8,128)(2,1)S(1)} %get-tuple-element.16.refs_9_), channel_id=1, source_target_pairs={{0,16},{16,0},{32,48},{48,32},{64,80},{80,64},{96,112},{112,96},{1... | collective-permute-start | bytes 811016 | tf_op jit(solution)/shard_map/ppermute | solution.py:23
  7.6 9.2 %collective-permute-start.1 = (bf16[1056,128]{1,0:T(8,128)(2,1)S(1)}, bf16[1056,128]{1,0:T(8,128)(2,1)S(1)}, u32[]{:S(2)}, u32[]{:S(2)}) collective-permute-start(bf16[1056,128]{1,0:T(8,128)(2,1)S(1)} %get-tuple-element.20), channel_id=1, source_target_pairs={{16,32},{32,16},{48,64},{64,48},{80,96},{96,80},{112,128},{128,112... | collective-permute-start | bytes 811016 | tf_op jit(solution)/shard_map/ppermute | solution.py:35
  17.0 12.2 %collective-permute-start.2 = (bf16[1056,128]{1,0:T(8,128)(2,1)S(1)}, bf16[1056,128]{1,0:T(8,128)(2,1)S(1)}, u32[]{:S(2)}, u32[]{:S(2)}) collective-permute-start(bf16[1056,128]{1,0:T(8,128)(2,1)S(1)} %get-tuple-element.24), channel_id=1, source_target_pairs={{1,2},{2,1},{3,4},{4,3},{5,6},{6,5},{7,8},{8,7},{9,10},{10,9},{11,... | collective-permute-start | bytes 811016 | tf_op jit(solution)/shard_map/ppermute | solution.py:23
  20.8 4.9 %collective-permute-start.3 = (bf16[1056,128]{1,0:T(8,128)(2,1)S(1)}, bf16[1056,128]{1,0:T(8,128)(2,1)S(1)}, u32[]{:S(2)}, u32[]{:S(2)}) collective-permute-start(bf16[1056,128]{1,0:T(8,128)(2,1)S(1)} %get-tuple-element.25), channel_id=1, source_target_pairs={{0,1},{1,0},{2,3},{3,2},{4,5},{5,4},{6,7},{7,6},{8,9},{9,8},{10,11... | collective-permute-start | bytes 811016 | tf_op jit(solution)/shard_map/ppermute | solution.py:23
  25.8 3.5 %copy-start = (bf16[4,8,64,128]{3,2,1,0:T(8,128)(2,1)S(1)}, bf16[4,8,64,128]{3,2,1,0:T(8,128)(2,1)}, u32[]{:S(2)}) copy-start(bf16[4,8,64,128]{3,2,1,0:T(8,128)(2,1)} %state_ref.1) | copy-start | bytes 1572868
